TPU v7x, 256 devices: a whole 4x4x8 slice. The times are simulated.
256 devices in a mesh: row: 32 (over z, x_lo, core), col: 8 (over x_hi, y).
Axes of the slice: x: 4 (x_hi: 2, x_lo: 2; x = x_hi * 2 + x_lo), y: 4, z: 8, core: 2. Of those that a mesh axis runs over, the one named last changes fastest.
Arguments:
- object_slices: float32 [2, 2, 3072, 768], P(None, None, 'row', 'col'), may hold values from -4 to 4
- probe: float32 [2, 192, 192], replicated, may hold values from -4 to 4
- propagator_phase: float32 [192, 192], replicated, may hold values from -3.140625 to 3.140625
- measured: float32 [32, 8, 2, 192, 192], P('row', 'col'), may hold values from 0 to 2
- offsets: int32 [32, 8, 2, 2], P('row', 'col'), may hold values from 0 to 95
- counts: int32 [32, 8], P('row', 'col'), may hold values from 1 to 2
Outputs:
- object_out: float32 [2, 2, 3072, 768], P(None, None, 'row', 'col')
- probe_out: float32 [2, 192, 192], replicated
Inputs may be any that keep to these rules, and one draw needn't show every extreme that they name: The slots below counts hold the tile's scan positions; the others are unused.
All inputs are finite; a program needn't handle non-finite values.
Results may differ from a plain program's by a relative error of at most 0.00014.
Values sent between devices are 32-bit elements; how exact they have to be, the bound alone decides.
A program may use at most 64 MiB of HBM per device.

v0:
```python
import math
import jax
import jax.numpy as jnp
from jax import lax
from jax.sharding import PartitionSpec as P

object_rate = 0.02
probe_rate = 0.3


def extended(cells, sides, width):
    for axis, dim in sides:
        count = lax.axis_size(axis)
        ends = count - 1
        head = lax.slice_in_dim(cells, 0, width, axis=dim)
        tail = lax.slice_in_dim(cells, cells.shape[dim] - width, cells.shape[dim], axis=dim)
        cells = jnp.concatenate(
            [
                lax.ppermute(tail, axis, [(i, (i + 1) % count) for i in range(ends)]),
                cells,
                lax.ppermute(head, axis, [((i + 1) % count, i) for i in range(ends)]),
            ],
            axis=dim,
        )
    return cells


def passed_along(x, axis, by):
    peers = lax.axis_size(axis)
    pairs = [(i, i + by) for i in range(peers) if 0 <= i + by < peers]
    return lax.ppermute(x, axis, pairs)


def times(a_real, a_imag, b_real, b_imag):
    return (a_real * b_real - a_imag * b_imag, a_real * b_imag + a_imag * b_real)


def times_conj(a_real, a_imag, b_real, b_imag):
    return (a_real * b_real + a_imag * b_imag, a_real * b_imag - a_imag * b_real)


def transform(x_real, x_imag, cosine, sine):
    highest = lax.Precision.HIGHEST

    def on_left(matrix, value):
        return jnp.einsum("jk,...kl->...jl", matrix, value, precision=highest)

    def on_right(value, matrix):
        return jnp.einsum("...jk,kl->...jl", value, matrix, precision=highest)

    mid_real = on_left(cosine, x_real) - on_left(sine, x_imag)
    mid_imag = on_left(cosine, x_imag) + on_left(sine, x_real)
    out_real = on_right(mid_real, cosine) - on_right(mid_imag, sine)
    out_imag = on_right(mid_imag, cosine) + on_right(mid_real, sine)
    return (out_real, out_imag)


def shards(object_slices, probe, propagator_phase, measured, offsets, counts):
    tile = object_slices.shape[-1]
    width = probe.shape[-1]
    slots = measured.shape[2]
    devices = lax.axis_size("row") * lax.axis_size("col")
    indices = jnp.arange(width, dtype=jnp.int32)
    products = indices[:, None] * indices[None, :] % width
    angles = products.astype(jnp.float32) * (2.0 * math.pi / width)
    norm_scale = 1.0 / math.sqrt(width)
    cosine = jnp.cos(angles) * norm_scale
    sine = jnp.sin(angles) * norm_scale
    minus_sine = -sine
    trans_real = jnp.cos(propagator_phase)
    trans_imag = jnp.sin(propagator_phase)
    intensities = measured[0, 0]
    starts = offsets[0, 0] + (tile - width // 2)
    live = counts[0, 0]
    zero = jnp.zeros((), jnp.int32)
    current = object_slices
    wave = probe
    padded = extended(current, (("row", 2), ("col", 3)), tile)
    wave_real = wave[0]
    wave_imag = wave[1]

    def process_position(row_offset, column_offset, measured_intensity):
        object_window = lax.dynamic_slice(
            padded, (zero, zero, row_offset, column_offset), (2, 2, width, width)
        )
        entry_real, entry_imag = times(
            wave_real, wave_imag, object_window[0, 0], object_window[0, 1]
        )
        spec_real, spec_imag = transform(entry_real, entry_imag, cosine, minus_sine)
        spec_real, spec_imag = times(trans_real, trans_imag, spec_real, spec_imag)
        carried_real, carried_imag = transform(spec_real, spec_imag, cosine, sine)
        leave_real, leave_imag = times(
            carried_real, carried_imag, object_window[1, 0], object_window[1, 1]
        )
        detector_real, detector_imag = transform(leave_real, leave_imag, cosine, minus_sine)
        amplitude_residual = (
            detector_real * detector_real + detector_imag * detector_imag - measured_intensity
        )
        back_real, back_imag = transform(
            amplitude_residual * detector_real, amplitude_residual * detector_imag, cosine, sine
        )
        second_real, second_imag = times_conj(carried_real, carried_imag, back_real, back_imag)
        before_real, before_imag = times_conj(
            object_window[1, 0], object_window[1, 1], back_real, back_imag
        )
        before_real, before_imag = transform(before_real, before_imag, cosine, minus_sine)
        before_real, before_imag = times_conj(trans_real, trans_imag, before_real, before_imag)
        inner_real, inner_imag = transform(before_real, before_imag, cosine, sine)
        first_real, first_imag = times_conj(wave_real, wave_imag, inner_real, inner_imag)
        grad_real, grad_imag = times_conj(
            object_window[0, 0], object_window[0, 1], inner_real, inner_imag
        )
        object_term = jnp.stack(
            [jnp.stack([first_real, first_imag]), jnp.stack([second_real, second_imag])]
        )
        return (object_term, jnp.stack([grad_real, grad_imag]))

    grad_pad = jnp.zeros(padded.shape, jnp.float32)
    wave_gradient = jnp.zeros(wave.shape, jnp.float32)
    object_terms, wave_terms = jax.vmap(process_position)(starts[:, 0], starts[:, 1], intensities)
    for slot in range(slots):
        position_weight = (slot < live).astype(jnp.float32)
        corner = (zero, zero, starts[slot, 0], starts[slot, 1])
        previous = lax.dynamic_slice(grad_pad, corner, (2, 2, width, width))
        grad_pad = lax.dynamic_update_slice(
            grad_pad, previous + position_weight * object_terms[slot], corner
        )
        wave_gradient = wave_gradient + position_weight * wave_terms[slot]
    from_right = passed_along(grad_pad[:, :, :, :tile], "col", -1)
    from_left = passed_along(grad_pad[:, :, :, 2 * tile :], "col", 1)
    folded = grad_pad[:, :, :, tile : 2 * tile] + from_right + from_left
    from_below = passed_along(folded[:, :, :tile], "row", -1)
    from_above = passed_along(folded[:, :, 2 * tile :], "row", 1)
    grad_object = folded[:, :, tile : 2 * tile] + from_below + from_above
    current = current - object_rate * grad_object
    rate = probe_rate / (slots * devices)
    total = lax.psum(wave_gradient, ("row", "col"))
    wave = wave - rate * total
    return (current, wave)


def solution(mesh):
    return jax.shard_map(
        shards,
        mesh=mesh,
        in_specs=(
            P(None, None, "row", "col"),
            P(),
            P(),
            P("row", "col", None, None, None),
            P("row", "col", None, None),
            P("row", "col"),
        ),
        out_specs=(P(None, None, "row", "col"), P()),
        check_vma=False,
    )
```

profile of v0, /device:TPU:1, one launch (start us, length us, event | category | flops | bytes accessed | tf_op | source)
XLA Modules:
  0.0 411.4 jit_solution(2080175894243225757)
XLA Ops:
  7.2 5.3 %collective-permute-start.1 = (f32[2,2,96,96]{3,2,1,0:T(8,128)}, f32[2,2,96,96]{3,2,1,0:T(8,128)S(1)}, u32[]{:S(2)}, u32[]{:S(2)}) collective-permute-start(f32[2,2,96,96]{3,2,1,0:T(8,128)} %param.6), channel_id=1, source_target_pairs={{8,0},{16,8},{24,16},{32,24},{40,32},{48,40},{56,48},{64,56},{72,6... | collective-permute-start | bytes 442376 | tf_op jit(solution)/shard_map/ppermute | solution.py:21
  12.5 1.9 collective-permute-start
  14.4 1.4 fusion.379
  21.6 1.6 fusion.378
  28.9 4.0 collective-permute-start.2
  33.0 10.8 %collective-permute-done.3 = f32[2,2,288,96]{3,2,1,0:T(8,128)S(1)} collective-permute-done((f32[2,2,288,96]{3,2,1,0:T(8,128)S(1)}, f32[2,2,288,96]{3,2,1,0:T(8,128)S(1)}, u32[]{:S(2)}, u32[]{:S(2)}) %collective-permute-start.3) | collective-permute-done | bytes 442400 | tf_op jit(solution)/shard_map/ppermute | solution.py:21
  45.4 6.7 %while.1 = (s32[]{:T(128)}, f32[2,2,288,288]{3,2,1,0:T(8,128)S(1)}, s32[2,4]{1,0:T(2,128)S(1)}, f32[2,2,2,192,192]{4,3,0,2,1:T(8,128)}, s32[]{:T(128)}) while((s32[]{:T(128)}, f32[2,2,288,288]{3,2,1,0:T(8,128)S(1)}, s32[2,4]{1,0:T(2,128)S(1)}, f32[2,2,2,192,192]{4,3,0,2,1:T(8,128)}, s32[]{:T(128)}) %tuple.40), condition=%wide.while_cond, body=%wide.while_body.sunk | while | flops 2 | bytes 1377405 | solution.py:83
  46.1 2.5 bitcast_dynamic-update-slice_fusion.2
  49.3 2.5 bitcast_dynamic-update-slice_fusion.2
  52.1 2.6 fusion.109
  54.6 2.4 fusion.105
  66.1 1.9 fusion.28
  68.0 1.3 convolution_add_fusion.9
  70.6 1.3 convolution_subtract_fusion.9
  78.3 1.5 convolution_subtract_fusion.7
  86.0 1.4 fusion.83
  87.4 1.4 fusion.87
  88.8 1.4 convolution_add_fusion.5
  91.4 1.6 convolution_subtract_fusion.5
  103.2 1.7 fusion.77
  107.3 1.3 fusion.14
  110.0 1.3 convolution_add_fusion.1
  112.6 1.3 convolution_subtract_fusion.1
  116.6 2.4 fusion.33
  120.2 7.7 %dynamic_update_slice.6 = f32[2,2,288,288]{3,2,1,0:T(8,128)S(1)} dynamic-update-slice(f32[2,2,288,288]{3,2,1,0:T(8,128)S(1)} %broadcast_in_dim.2, f32[2,2,192,192]{3,2,1,0:T(8,128)} %fusion.7, s32[]{:T(128)} %constant.13.clone.1, s32[]{:T(128)} %constant.13.clone.1, s32[]{:T(128)S(6)} %select_n.126, s32[]{:T(128)S(6)} %select_n.127) | dynamic-update-slice | bytes 1179652 | tf_op jit(solution)/shard_map/dynamic_update_slice | solution.py:125
  129.1 7.5 %dynamic_update_slice.7 = f32[2,2,288,288]{3,2,1,0:T(8,128)S(1)} dynamic-update-slice(f32[2,2,288,288]{3,2,1,0:T(8,128)S(1)} %dynamic_update_slice.6, f32[2,2,192,192]{3,2,1,0:T(8,128)} %fusion.10, s32[]{:T(128)} %constant.13.clone.1, s32[]{:T(128)} %constant.13.clone.1, s32[]{:T(128)S(6)} %select_n.128, s32[]{:T(128)S(6)} %select_n.129) | dynamic-update-slice | bytes 1179652 | tf_op jit(solution)/shard_map/dynamic_update_slice | solution.py:125
  138.9 5.8 %collective-permute-start.5 = (f32[2,2,288,96]{3,2,1,0:T(8,128)S(1)}, f32[2,2,288,96]{3,2,1,0:T(8,128)}, u32[]{:S(2)}, u32[]{:S(2)}) collective-permute-start(f32[2,2,288,96]{3,2,1,0:T(8,128)S(1)} %get-tuple-element.27), channel_id=1, source_target_pairs={{0,1},{1,2},{2,3},{3,4},{4,5},{5,6},{6,7},{8,9},{9,10},{10,11},{11... | collective-permute-start | bytes 1327112 | tf_op jit(solution)/shard_map/ppermute | solution.py:31
  145.7 8.6 %collective-permute-done.4 = f32[2,2,288,96]{3,2,1,0:T(8,128)S(1)} collective-permute-done((f32[2,2,288,96]{3,2,1,0:T(8,128)}, f32[2,2,288,96]{3,2,1,0:T(8,128)S(1)}, u32[]{:S(2)}, u32[]{:S(2)}) %collective-permute-start.4) | collective-permute-done | bytes 442400 | tf_op jit(solution)/shard_map/ppermute | solution.py:31
  156.3 4.5 %collective-permute-start.6 = (f32[2,2,96,96]{3,2,1,0:T(8,128)S(1)}, f32[2,2,96,96]{3,2,1,0:T(8,128)S(1)}, u32[]{:S(2)}, u32[]{:S(2)}) collective-permute-start(f32[2,2,96,96]{3,2,1,0:T(8,128)S(1)} %get-tuple-element.34), channel_id=1, source_target_pairs={{8,0},{16,8},{24,16},{32,24},{40,32},{48,40},{56,48},{64,56},{72,6... | collective-permute-start | bytes 442376 | tf_op jit(solution)/shard_map/ppermute | solution.py:31
  160.9 3.5 collective-permute-start.7
  164.4 237.5 %all-reduce.2.cloned.1.call-done = f32[2,192,192]{2,1,0:T(8,128)} async-done(((f32[2,192,192]{2,1,0:T(8,128)}), f32[2,192,192]{2,1,0:T(8,128)}) %all-reduce.2.cloned.1.call-update) | async-done | bytes 294928 | tf_op jit(solution)/shard_map/psum | solution.py:137
  401.9 1.8 multiply_subtract_fusion
  (83 shorter events, 56.2 us)
Async XLA Ops:
  7.2 25.8 %copy-start.4 = (f32[2,192,192]{2,1,0:T(8,128)S(1)}, f32[2,192,192]{2,1,0:T(8,128)}, u32[]{:S(2)}) copy-start(f32[2,192,192]{2,1,0:T(8,128)} %param.7) | copy-start | bytes 884740
  7.2 394.7 %all-reduce.2.cloned.1.call-start = ((), (), s32[]{:S(2)}) async-start(), calls=%async_computation | async-start | bytes 786432 | tf_op jit(solution)/shard_map/psum | solution.py:137
  7.2 20.3 %collective-permute-start.1 = (f32[2,2,96,96]{3,2,1,0:T(8,128)}, f32[2,2,96,96]{3,2,1,0:T(8,128)S(1)}, u32[]{:S(2)}, u32[]{:S(2)}) collective-permute-start(f32[2,2,96,96]{3,2,1,0:T(8,128)} %param.6), channel_id=1, source_target_pairs={{8,0},{16,8},{24,16},{32,24},{40,32},{48,40},{56,48},{64,56},{72,6... | collective-permute-start | bytes 442376 | tf_op jit(solution)/shard_map/ppermute | solution.py:21
  12.5 14.0 %collective-permute-start = (f32[2,2,96,96]{3,2,1,0:T(8,128)}, f32[2,2,96,96]{3,2,1,0:T(8,128)S(1)}, u32[]{:S(2)}, u32[]{:S(2)}) collective-permute-start(f32[2,2,96,96]{3,2,1,0:T(8,128)} %param.6), channel_id=1, source_target_pairs={{0,8},{8,16},{16,24},{24,32},{32,40},{40,48},{48,56},{56,64},{64,7... | collective-permute-start | bytes 442376 | tf_op jit(solution)/shard_map/ppermute | solution.py:19
  27.6 16.3 %collective-permute-start.3 = (f32[2,2,288,96]{3,2,1,0:T(8,128)S(1)}, f32[2,2,288,96]{3,2,1,0:T(8,128)S(1)}, u32[]{:S(2)}, u32[]{:S(2)}) collective-permute-start(f32[2,2,288,96]{3,2,1,0:T(8,128)S(1)} %constant_dynamic-update-slice_fusion), channel_id=1, source_target_pairs={{1,0},{2,1},{3,2},{4,3},{5,4},{6,5},{7,6},{9,8},{10,9},{11,10},{12... | collective-permute-start | bytes 1327112 | tf_op jit(solution)/shard_map/ppermute | solution.py:21
  28.9 15.8 %collective-permute-start.2 = (f32[2,2,288,96]{3,2,1,0:T(8,128)S(1)}, f32[2,2,288,96]{3,2,1,0:T(8,128)S(1)}, u32[]{:S(2)}, u32[]{:S(2)}) collective-permute-start(f32[2,2,288,96]{3,2,1,0:T(8,128)S(1)} %constant_dynamic-update-slice_fusion), channel_id=1, source_target_pairs={{0,1},{1,2},{2,3},{3,4},{4,5},{5,6},{6,7},{8,9},{9,10},{10,11},{11... | collective-permute-start | bytes 1327112 | tf_op jit(solution)/shard_map/ppermute | solution.py:19
  52.1 5.0 %copy-start.1 = (f32[2,2,2,192,192]{4,3,0,2,1:T(8,128)S(1)}, f32[2,2,2,192,192]{4,3,0,2,1:T(8,128)}, u32[]{:S(2)}) copy-start(f32[2,2,2,192,192]{4,3,0,2,1:T(8,128)} %get-tuple-element.9) | copy-start | bytes 3538948
  82.3 3.8 copy-start
  136.6 8.2 %copy-start.2 = (f32[1,2,192,192]{3,2,1,0:T(8,128)S(1)}, f32[1,2,192,192]{3,2,1,0:T(8,128)}, u32[]{:S(2)}) copy-start(f32[1,2,192,192]{3,2,1,0:T(8,128)} %get-tuple-element.20) | copy-start | bytes 884740
  136.6 8.2 %copy-start.3 = (f32[1,2,192,192]{3,2,1,0:T(8,128)S(1)}, f32[1,2,192,192]{3,2,1,0:T(8,128)}, u32[]{:S(2)}) copy-start(f32[1,2,192,192]{3,2,1,0:T(8,128)} %get-tuple-element.21) | copy-start | bytes 884740
  137.7 16.6 %collective-permute-start.4 = (f32[2,2,288,96]{3,2,1,0:T(8,128)}, f32[2,2,288,96]{3,2,1,0:T(8,128)S(1)}, u32[]{:S(2)}, u32[]{:S(2)}) collective-permute-start(f32[2,2,288,96]{3,2,1,0:T(8,128)} %get-tuple-element.26), channel_id=1, source_target_pairs={{1,0},{2,1},{3,2},{4,3},{5,4},{6,5},{7,6},{9,8},{10,9},{11,10},{12... | collective-permute-start | bytes 1327112 | tf_op jit(solution)/shard_map/ppermute | solution.py:31
  138.9 16.0 %collective-permute-start.5 = (f32[2,2,288,96]{3,2,1,0:T(8,128)S(1)}, f32[2,2,288,96]{3,2,1,0:T(8,128)}, u32[]{:S(2)}, u32[]{:S(2)}) collective-permute-start(f32[2,2,288,96]{3,2,1,0:T(8,128)S(1)} %get-tuple-element.27), channel_id=1, source_target_pairs={{0,1},{1,2},{2,3},{3,4},{4,5},{5,6},{6,7},{8,9},{9,10},{10,11},{11... | collective-permute-start | bytes 1327112 | tf_op jit(solution)/shard_map/ppermute | solution.py:31
  145.7 256.2 %copy-start.5 = (f32[2,192,192]{2,1,0:T(8,128)S(1)}, f32[2,192,192]{2,1,0:T(8,128)}, u32[]{:S(2)}) copy-start(f32[2,192,192]{2,1,0:T(8,128)} %param.7) | copy-start | bytes 884740
  156.3 247.4 %copy-start.6 = (f32[2,2,96,96]{3,2,1,0:T(8,128)S(1)}, f32[2,2,96,96]{3,2,1,0:T(8,128)}, u32[]{:S(2)}) copy-start(f32[2,2,96,96]{3,2,1,0:T(8,128)} %param.6) | copy-start | bytes 442372
  156.3 247.4 %collective-permute-start.6 = (f32[2,2,96,96]{3,2,1,0:T(8,128)S(1)}, f32[2,2,96,96]{3,2,1,0:T(8,128)S(1)}, u32[]{:S(2)}, u32[]{:S(2)}) collective-permute-start(f32[2,2,96,96]{3,2,1,0:T(8,128)S(1)} %get-tuple-element.34), channel_id=1, source_target_pairs={{8,0},{16,8},{24,16},{32,24},{40,32},{48,40},{56,48},{64,56},{72,6... | collective-permute-start | bytes 442376 | tf_op jit(solution)/shard_map/ppermute | solution.py:31
  160.9 242.8 %collective-permute-start.7 = (f32[2,2,96,96]{3,2,1,0:T(8,128)S(1)}, f32[2,2,96,96]{3,2,1,0:T(8,128)S(1)}, u32[]{:S(2)}, u32[]{:S(2)}) collective-permute-start(f32[2,2,96,96]{3,2,1,0:T(8,128)S(1)} %get-tuple-element.35), channel_id=1, source_target_pairs={{0,8},{8,16},{16,24},{24,32},{32,40},{40,48},{48,56},{56,64},{64,7... | collective-permute-start | bytes 442376 | tf_op jit(solution)/shard_map/ppermute | solution.py:31
Sparse Core Ops, SparseCore 0:
  145.8 256.0 all-reduce.1
where the time goes:
time: 415 us; the launch traced here: 411 us
  waiting for transfers between devices  259 us (62%)
  matrix products  66.4 us (16%)
  starting transfers between devices  27.7 us (7%)
  local copies, waits for them, and re-layouts  26.9 us (6%)
  between operations  23 us (6%)
  other arithmetic  8.57 us (2%)
    psum x1, waiting for transfers between devices, shards(): total = lax.psum(wave_gradient, ('row', 'col'))  237 us
    dot_general x24, matrix products, on_left(): return jnp.einsum('jk,...kl->...jl', matrix, value, precision=highest)  35 us
    dot_general x24, matrix products, on_right(): return jnp.einsum('...jk,kl->...jl', value, matrix, precision=highest)  31.4 us
    dynamic_update_slice x2, local copies, waits for them, and re-layouts, shards(): lax.dynamic_update_slice(grad_pad, previous + position_weight * object_te...  15.2 us
    ppermute x4, starting transfers between devices, passed_along(): return lax.ppermute(x, axis, pairs)  15.2 us
    ppermute x2, waiting for transfers between devices, extended(): lax.ppermute(head, axis, [((i + 1) % count, i) for i in range(ends)])  10.8 us
    ppermute x4, waiting for transfers between devices, passed_along(): return lax.ppermute(x, axis, pairs)  9.3 us
  transfers between devices with their start and end apart: 9, of which 5 were waited for; matrix products, arithmetic and copies ran while one was open for 2% of the time, Pallas kernels for 0%

commit v1 on v0

--- a/solution.py
+++ b/solution.py
@@ -134,7 +134,7 @@
     grad_object = folded[:, :, tile : 2 * tile] + from_below + from_above
     current = current - object_rate * grad_object
     rate = probe_rate / (slots * devices)
-    total = lax.psum(wave_gradient, ("row", "col"))
+    total = lax.psum(lax.psum(wave_gradient, "row"), "col")
     wave = wave - rate * total
     return (current, wave)
 

time: 415 us -> 475 us (1.14)
  waiting for transfers between devices: 259 us -> 315 us
    psum x1 -> x2, waiting for transfers between devices: 237 us -> 304 us  [shards(): total = lax.psum(lax.psum(wave_gradient, 'row'), 'col')]
    ppermute x4, waiting for transfers between devices: 9.3 us -> 0.01 us  [passed_along(): return lax.ppermute(x, axis, pairs)]
  transfers between devices with their start and end apart: 9 -> 10, of which waited for: 5 -> 4; matrix products, arithmetic and copies ran while one was open for 2% -> 2% of each run, Pallas kernels for 0% -> 0%
where the time goes in v1:
time: 475 us; the launch traced here: 467 us
  waiting for transfers between devices  315 us (66%)
  matrix products  66.4 us (14%)
  local copies, waits for them, and re-layouts  26.9 us (6%)
  starting transfers between devices  26.2 us (6%)
  between operations  23.1 us (5%)
  other arithmetic  8.62 us (2%)
    psum x2, waiting for transfers between devices, shards(): total = lax.psum(lax.psum(wave_gradient, 'row'), 'col')  304 us
    dot_general x24, matrix products, on_left(): return jnp.einsum('jk,...kl->...jl', matrix, value, precision=highest)  35 us
    dot_general x24, matrix products, on_right(): return jnp.einsum('...jk,kl->...jl', value, matrix, precision=highest)  31.4 us
    dynamic_update_slice x2, local copies, waits for them, and re-layouts, shards(): lax.dynamic_update_slice(grad_pad, previous + position_weight * object_te...  15.2 us
    ppermute x4, starting transfers between devices, passed_along(): return lax.ppermute(x, axis, pairs)  13.6 us
    ppermute x2, waiting for transfers between devices, extended(): lax.ppermute(head, axis, [((i + 1) % count, i) for i in range(ends)])  10.8 us
  transfers between devices with their start and end apart: 10, of which 4 were waited for; matrix products, arithmetic and copies ran while one was open for 2% of the time, Pallas kernels for 0%

profile of v1, /device:TPU:1, one launch (start us, length us, event | category | flops | bytes accessed | tf_op | source)
XLA Modules:
  0.0 466.8 jit_solution(11702991375085324433)
XLA Ops:
  7.2 5.3 %collective-permute-start.1 = (f32[2,2,96,96]{3,2,1,0:T(8,128)}, f32[2,2,96,96]{3,2,1,0:T(8,128)S(1)}, u32[]{:S(2)}, u32[]{:S(2)}) collective-permute-start(f32[2,2,96,96]{3,2,1,0:T(8,128)} %param.6), channel_id=1, source_target_pairs={{8,0},{16,8},{24,16},{32,24},{40,32},{48,40},{56,48},{64,56},{72,6... | collective-permute-start | bytes 442376 | tf_op jit(solution)/shard_map/ppermute | solution.py:21
  12.5 1.9 collective-permute-start
  14.4 1.4 fusion.379
  21.6 1.6 fusion.378
  28.9 4.0 collective-permute-start.2
  33.0 10.8 %collective-permute-done.3 = f32[2,2,288,96]{3,2,1,0:T(8,128)S(1)} collective-permute-done((f32[2,2,288,96]{3,2,1,0:T(8,128)S(1)}, f32[2,2,288,96]{3,2,1,0:T(8,128)S(1)}, u32[]{:S(2)}, u32[]{:S(2)}) %collective-permute-start.3) | collective-permute-done | bytes 442400 | tf_op jit(solution)/shard_map/ppermute | solution.py:21
  45.4 6.7 %while.1 = (s32[]{:T(128)}, f32[2,2,288,288]{3,2,1,0:T(8,128)S(1)}, s32[2,4]{1,0:T(2,128)S(1)}, f32[2,2,2,192,192]{4,3,0,2,1:T(8,128)}, s32[]{:T(128)}) while((s32[]{:T(128)}, f32[2,2,288,288]{3,2,1,0:T(8,128)S(1)}, s32[2,4]{1,0:T(2,128)S(1)}, f32[2,2,2,192,192]{4,3,0,2,1:T(8,128)}, s32[]{:T(128)}) %tuple.40), condition=%wide.while_cond, body=%wide.while_body.sunk | while | flops 2 | bytes 1377405 | solution.py:83
  46.1 2.5 bitcast_dynamic-update-slice_fusion.2
  49.3 2.5 bitcast_dynamic-update-slice_fusion.2
  52.1 2.6 fusion.109
  54.6 2.4 fusion.105
  66.1 1.9 fusion.28
  68.0 1.3 convolution_add_fusion.9
  70.6 1.3 convolution_subtract_fusion.9
  78.3 1.5 convolution_subtract_fusion.7
  86.0 1.4 fusion.83
  87.4 1.4 fusion.87
  88.8 1.4 convolution_add_fusion.5
  91.4 1.6 convolution_subtract_fusion.5
  103.2 1.7 fusion.77
  107.3 1.3 fusion.14
  110.0 1.3 convolution_add_fusion.1
  112.6 1.3 convolution_subtract_fusion.1
  116.7 2.4 fusion.33
  120.2 7.7 %dynamic_update_slice.6 = f32[2,2,288,288]{3,2,1,0:T(8,128)S(1)} dynamic-update-slice(f32[2,2,288,288]{3,2,1,0:T(8,128)S(1)} %broadcast_in_dim.2, f32[2,2,192,192]{3,2,1,0:T(8,128)} %fusion.7, s32[]{:T(128)} %constant.13.clone.1, s32[]{:T(128)} %constant.13.clone.1, s32[]{:T(128)S(6)} %select_n.126, s32[]{:T(128)S(6)} %select_n.127) | dynamic-update-slice | bytes 1179652 | tf_op jit(solution)/shard_map/dynamic_update_slice | solution.py:125
  129.1 7.5 %dynamic_update_slice.7 = f32[2,2,288,288]{3,2,1,0:T(8,128)S(1)} dynamic-update-slice(f32[2,2,288,288]{3,2,1,0:T(8,128)S(1)} %dynamic_update_slice.6, f32[2,2,192,192]{3,2,1,0:T(8,128)} %fusion.10, s32[]{:T(128)} %constant.13.clone.1, s32[]{:T(128)} %constant.13.clone.1, s32[]{:T(128)S(6)} %select_n.128, s32[]{:T(128)S(6)} %select_n.129) | dynamic-update-slice | bytes 1179652 | tf_op jit(solution)/shard_map/dynamic_update_slice | solution.py:125
  139.0 5.8 %collective-permute-start.5 = (f32[2,2,288,96]{3,2,1,0:T(8,128)S(1)}, f32[2,2,288,96]{3,2,1,0:T(8,128)}, u32[]{:S(2)}, u32[]{:S(2)}) collective-permute-start(f32[2,2,288,96]{3,2,1,0:T(8,128)S(1)} %get-tuple-element.27), channel_id=1, source_target_pairs={{0,1},{1,2},{2,3},{3,4},{4,5},{5,6},{6,7},{8,9},{9,10},{10,11},{11... | collective-permute-start | bytes 1327112 | tf_op jit(solution)/shard_map/ppermute | solution.py:31
  145.8 221.2 %all-reduce.3.cloned.1.call-done = f32[2,192,192]{2,1,0:T(8,128)} async-done(((f32[2,192,192]{2,1,0:T(8,128)}), f32[2,192,192]{2,1,0:T(8,128)}) %all-reduce.3.cloned.1.call-update) | async-done | bytes 294928 | tf_op jit(solution)/shard_map/psum | solution.py:137
  368.4 4.6 collective-permute-start.6
  373.0 1.9 collective-permute-start.7
  374.9 82.3 %all-reduce.5.cloned.1.call-done = f32[2,192,192]{2,1,0:T(8,128)} async-done(((f32[2,192,192]{2,1,0:T(8,128)}), f32[2,192,192]{2,1,0:T(8,128)}) %all-reduce.5.cloned.1.call-update) | async-done | bytes 294928 | tf_op jit(solution)/shard_map/psum | solution.py:137
  457.3 1.8 multiply_subtract_fusion
  (86 shorter events, 55.6 us)
Async XLA Ops:
  7.2 25.8 %copy-start.4 = (f32[2,192,192]{2,1,0:T(8,128)S(1)}, f32[2,192,192]{2,1,0:T(8,128)}, u32[]{:S(2)}) copy-start(f32[2,192,192]{2,1,0:T(8,128)} %param.7) | copy-start | bytes 884740
  7.2 359.8 %all-reduce.3.cloned.1.call-start = ((), (), s32[]{:S(2)}) async-start(), calls=%async_computation | async-start | bytes 786432 | tf_op jit(solution)/shard_map/psum | solution.py:137
  7.2 20.3 %collective-permute-start.1 = (f32[2,2,96,96]{3,2,1,0:T(8,128)}, f32[2,2,96,96]{3,2,1,0:T(8,128)S(1)}, u32[]{:S(2)}, u32[]{:S(2)}) collective-permute-start(f32[2,2,96,96]{3,2,1,0:T(8,128)} %param.6), channel_id=1, source_target_pairs={{8,0},{16,8},{24,16},{32,24},{40,32},{48,40},{56,48},{64,56},{72,6... | collective-permute-start | bytes 442376 | tf_op jit(solution)/shard_map/ppermute | solution.py:21
  12.5 14.0 %collective-permute-start = (f32[2,2,96,96]{3,2,1,0:T(8,128)}, f32[2,2,96,96]{3,2,1,0:T(8,128)S(1)}, u32[]{:S(2)}, u32[]{:S(2)}) collective-permute-start(f32[2,2,96,96]{3,2,1,0:T(8,128)} %param.6), channel_id=1, source_target_pairs={{0,8},{8,16},{16,24},{24,32},{32,40},{40,48},{48,56},{56,64},{64,7... | collective-permute-start | bytes 442376 | tf_op jit(solution)/shard_map/ppermute | solution.py:19
  27.6 16.3 %collective-permute-start.3 = (f32[2,2,288,96]{3,2,1,0:T(8,128)S(1)}, f32[2,2,288,96]{3,2,1,0:T(8,128)S(1)}, u32[]{:S(2)}, u32[]{:S(2)}) collective-permute-start(f32[2,2,288,96]{3,2,1,0:T(8,128)S(1)} %constant_dynamic-update-slice_fusion), channel_id=1, source_target_pairs={{1,0},{2,1},{3,2},{4,3},{5,4},{6,5},{7,6},{9,8},{10,9},{11,10},{12... | collective-permute-start | bytes 1327112 | tf_op jit(solution)/shard_map/ppermute | solution.py:21
  28.9 15.8 %collective-permute-start.2 = (f32[2,2,288,96]{3,2,1,0:T(8,128)S(1)}, f32[2,2,288,96]{3,2,1,0:T(8,128)S(1)}, u32[]{:S(2)}, u32[]{:S(2)}) collective-permute-start(f32[2,2,288,96]{3,2,1,0:T(8,128)S(1)} %constant_dynamic-update-slice_fusion), channel_id=1, source_target_pairs={{0,1},{1,2},{2,3},{3,4},{4,5},{5,6},{6,7},{8,9},{9,10},{10,11},{11... | collective-permute-start | bytes 1327112 | tf_op jit(solution)/shard_map/ppermute | solution.py:19
  52.1 5.0 %copy-start.1 = (f32[2,2,2,192,192]{4,3,0,2,1:T(8,128)S(1)}, f32[2,2,2,192,192]{4,3,0,2,1:T(8,128)}, u32[]{:S(2)}) copy-start(f32[2,2,2,192,192]{4,3,0,2,1:T(8,128)} %get-tuple-element.9) | copy-start | bytes 3538948
  82.3 3.8 copy-start
  136.6 8.2 %copy-start.2 = (f32[1,2,192,192]{3,2,1,0:T(8,128)S(1)}, f32[1,2,192,192]{3,2,1,0:T(8,128)}, u32[]{:S(2)}) copy-start(f32[1,2,192,192]{3,2,1,0:T(8,128)} %get-tuple-element.20) | copy-start | bytes 884740
  136.7 8.2 %copy-start.3 = (f32[1,2,192,192]{3,2,1,0:T(8,128)S(1)}, f32[1,2,192,192]{3,2,1,0:T(8,128)}, u32[]{:S(2)}) copy-start(f32[1,2,192,192]{3,2,1,0:T(8,128)} %get-tuple-element.21) | copy-start | bytes 884740
  137.7 229.3 %collective-permute-start.4 = (f32[2,2,288,96]{3,2,1,0:T(8,128)}, f32[2,2,288,96]{3,2,1,0:T(8,128)S(1)}, u32[]{:S(2)}, u32[]{:S(2)}) collective-permute-start(f32[2,2,288,96]{3,2,1,0:T(8,128)} %get-tuple-element.26), channel_id=1, source_target_pairs={{1,0},{2,1},{3,2},{4,3},{5,4},{6,5},{7,6},{9,8},{10,9},{11,10},{12... | collective-permute-start | bytes 1327112 | tf_op jit(solution)/shard_map/ppermute | solution.py:31
  139.0 228.0 %collective-permute-start.5 = (f32[2,2,288,96]{3,2,1,0:T(8,128)S(1)}, f32[2,2,288,96]{3,2,1,0:T(8,128)}, u32[]{:S(2)}, u32[]{:S(2)}) collective-permute-start(f32[2,2,288,96]{3,2,1,0:T(8,128)S(1)} %get-tuple-element.27), channel_id=1, source_target_pairs={{0,1},{1,2},{2,3},{3,4},{4,5},{5,6},{6,7},{8,9},{9,10},{10,11},{11... | collective-permute-start | bytes 1327112 | tf_op jit(solution)/shard_map/ppermute | solution.py:31
  145.7 311.6 %all-reduce.5.cloned.1.call-start = ((), (), s32[]{:S(2)}) async-start(), calls=%async_computation.1 | async-start | bytes 786432 | tf_op jit(solution)/shard_map/psum | solution.py:137
  367.0 90.3 %copy-start.5 = (f32[2,192,192]{2,1,0:T(8,128)S(1)}, f32[2,192,192]{2,1,0:T(8,128)}, u32[]{:S(2)}) copy-start(f32[2,192,192]{2,1,0:T(8,128)} %param.7) | copy-start | bytes 884740
  368.4 90.7 %copy-start.6 = (f32[2,2,96,96]{3,2,1,0:T(8,128)S(1)}, f32[2,2,96,96]{3,2,1,0:T(8,128)}, u32[]{:S(2)}) copy-start(f32[2,2,96,96]{3,2,1,0:T(8,128)} %param.6) | copy-start | bytes 442372
  368.4 90.7 %collective-permute-start.6 = (f32[2,2,96,96]{3,2,1,0:T(8,128)S(1)}, f32[2,2,96,96]{3,2,1,0:T(8,128)S(1)}, u32[]{:S(2)}, u32[]{:S(2)}) collective-permute-start(f32[2,2,96,96]{3,2,1,0:T(8,128)S(1)} %get-tuple-element.34), channel_id=1, source_target_pairs={{8,0},{16,8},{24,16},{32,24},{40,32},{48,40},{56,48},{64,56},{72,6... | collective-permute-start | bytes 442376 | tf_op jit(solution)/shard_map/ppermute | solution.py:31
  373.0 86.1 %collective-permute-start.7 = (f32[2,2,96,96]{3,2,1,0:T(8,128)S(1)}, f32[2,2,96,96]{3,2,1,0:T(8,128)S(1)}, u32[]{:S(2)}, u32[]{:S(2)}) collective-permute-start(f32[2,2,96,96]{3,2,1,0:T(8,128)S(1)} %get-tuple-element.35), channel_id=1, source_target_pairs={{0,8},{8,16},{16,24},{24,32},{32,40},{40,48},{48,56},{56,64},{64,7... | collective-permute-start | bytes 442376 | tf_op jit(solution)/shard_map/ppermute | solution.py:31
Sparse Core Ops, SparseCore 0:
  145.8 221.0 all-reduce.2
  369.8 87.4 all-reduce.4
